TPU v7x, 32 devices: a whole 2x2x4 slice. The times are simulated.
32 devices in a mesh: tm: 4 (over x, core), rows: 8 (over z, y).
Axes of the slice: x: 2, y: 2, z: 4, core: 2. Of those that a mesh axis runs over, the one named last changes fastest.
Arguments:
- video: bfloat16 [8, 16, 128, 128], P('tm', 'rows'), may hold values from -6 to 6
- kernel: bfloat16 [3, 3, 3, 128, 128], replicated, may hold values from -0.109375 to 0.109375
- cotangent: bfloat16 [8, 16, 128, 128], P('tm', 'rows'), may hold values from -6 to 6
Outputs:
- activated: bfloat16 [8, 16, 128, 128], P('tm', 'rows')
- input_grad: bfloat16 [8, 16, 128, 128], P('tm', 'rows')
- kernel_grad: float32 [128, 3456], P('rows', 'tm')
All inputs are finite; a program needn't handle non-finite values.
Results may differ from a plain program's by a relative error of at most 0.0049.
Values may be sent and summed in bfloat16 or wider, within the bound.
A program may use at most 64 MiB of HBM per device.

v0:
```python
import jax
import jax.numpy as jnp
from jax import lax
from jax.sharding import PartitionSpec as P


def passed_along(x, axis, by):
    devices = lax.axis_size(axis)
    pairs = [(i, i + by) for i in range(devices) if 0 <= i + by < devices]
    return lax.ppermute(x, axis, pairs)


def padded(block, sides, width):
    for axis, dim in sides:
        count = lax.axis_size(axis)
        forward = [(i, i + 1) for i in range(count - 1)]
        backward = [(target, source) for source, target in forward]
        low = lax.ppermute(
            lax.slice_in_dim(block, block.shape[dim] - width, None, axis=dim), axis, forward
        )
        high = lax.ppermute(lax.slice_in_dim(block, 0, width, axis=dim), axis, backward)
        block = jnp.concatenate([low, block, high], axis=dim)
    return block


def make_patches(extended):
    frames = extended.shape[0] - 2
    height = extended.shape[1] - 2
    width = extended.shape[2]
    chans = extended.shape[3]
    wide = jnp.pad(extended, ((0, 0), (0, 0), (1, 1), (0, 0)))
    patches = []
    for a in range(3):
        for b in range(3):
            parts = [wide[a : a + frames, b : b + height, c : c + width] for c in range(3)]
            patches.append(
                jnp.concatenate(parts, axis=-1).reshape(frames * height * width, 3 * chans)
            )
    return patches


def apply_taps(patches, kmat):
    total = jnp.dot(patches[0], kmat[0, 0], preferred_element_type=jnp.float32)
    for index in range(1, 9):
        total = total + jnp.dot(
            patches[index], kmat[index // 3, index % 3], preferred_element_type=jnp.float32
        )
    return total


def local(video, kernel, cotangent):
    frames, height, width, chans = video.shape
    forward_mat = kernel.reshape(3, 3, 3 * chans, chans)
    earlier = passed_along(video, "tm", 1)
    extended = padded(jnp.concatenate([earlier, video], axis=0), (("rows", 1),), 1)
    patches = make_patches(extended)
    pre = apply_taps(patches, forward_mat)
    sig = 1.0 / (1.0 + jnp.exp(-pre))
    activated = (pre * sig).astype(jnp.bfloat16).reshape(frames, height, width, chans)
    grad_flat = cotangent.reshape(frames * height * width, chans).astype(jnp.float32)
    pre_grad = (grad_flat * sig * (1.0 + pre * (1.0 - sig))).astype(jnp.bfloat16)
    pre_grid = pre_grad.reshape(frames, height, width, chans)
    later = passed_along(pre_grid, "tm", -1)
    grad_ext = padded(jnp.concatenate([pre_grid, later], axis=0), (("rows", 1),), 1)
    flipped = jnp.transpose(kernel[::-1, ::-1, ::-1], (0, 1, 2, 4, 3)).reshape(
        3, 3, 3 * chans, chans
    )
    input_grad = (
        apply_taps(make_patches(grad_ext), flipped)
        .astype(jnp.bfloat16)
        .reshape(frames, height, width, chans)
    )
    blocks = [
        lax.dot_general(
            pre_grad, piece, (((0,), (0,)), ((), ())), preferred_element_type=jnp.float32
        )
        for piece in patches
    ]
    partial_grad = jnp.concatenate(blocks, axis=1)
    owned = lax.psum_scatter(partial_grad, "rows", scatter_dimension=0, tiled=True)
    kernel_grad = lax.psum_scatter(owned, "tm", scatter_dimension=1, tiled=True)
    return (activated, input_grad, kernel_grad)


def solution(mesh):
    in_specs = (P("tm", "rows", None, None), P(), P("tm", "rows", None, None))
    out_specs = (P("tm", "rows", None, None), P("tm", "rows", None, None), P("rows", "tm"))
    return jax.shard_map(local, mesh=mesh, in_specs=in_specs, out_specs=out_specs, check_vma=False)
```

profile of v0, /device:TPU:0, one launch (start us, length us, event | category | flops | bytes accessed | tf_op | source)
XLA Modules:
  0.0 157.5 jit_solution(9117602661084998378)
XLA Ops:
  7.2 2.4 %collective-permute-start = (bf16[2,2,128,128]{3,2,1,0:T(8,128)(2,1)}, bf16[2,2,128,128]{3,2,1,0:T(8,128)(2,1)S(1)}, u32[]{:S(2)}, u32[]{:S(2)}) collective-permute-start(bf16[2,2,128,128]{3,2,1,0:T(8,128)(2,1)} %param.3), channel_id=1, source_target_pairs={{0,8},{8,16},{16,24},{1,9},{9,17},{17,25},{2,10},{10,18},{18,26},{... | collective-permute-start | bytes 393224 | tf_op jit(solution)/shard_map/ppermute | solution.py:10
  9.6 1.2 collective-permute-done
  10.8 0.9 constant_dynamic-update-slice_fusion
  11.7 4.3 %collective-permute-start.1 = (bf16[4,1,128,128]{3,2,1,0:T(8,128)(2,1)S(1)}, bf16[4,1,128,128]{3,2,1,0:T(8,128)(2,1)S(1)}, u32[]{:S(2)}, u32[]{:S(2)}) collective-permute-start(bf16[4,1,128,128]{3,2,1,0:T(8,128)(2,1)S(1)} %get-tuple-element.60), channel_id=1, source_target_pairs={{0,1},{1,2},{2,3},{3,4},{4,5},{5,6},{6,7},{8,9},{9,10},{10,11},{11... | collective-permute-start | bytes 393224 | tf_op jit(solution)/shard_map/ppermute | solution.py:18
  16.0 1.3 collective-permute-start.2
  17.3 2.0 %copy.7 = bf16[3,3,3,128,128]{3,4,2,1,0:T(8,128)(2,1)S(1)} copy(bf16[3,3,3,128,128]{4,3,2,1,0:T(8,128)(2,1)} %param.4) | data formatting | bytes 1769472 | tf_op args[1]
  19.4 3.5 %collective-permute-done.2 = bf16[4,1,128,128]{3,2,1,0:T(8,128)(2,1)S(1)} collective-permute-done((bf16[4,1,128,128]{3,2,1,0:T(8,128)(2,1)S(1)}, bf16[4,1,128,128]{3,2,1,0:T(8,128)(2,1)S(1)}, u32[]{:S(2)}, u32[]{:S(2)}) %collective-permute-start.2) | collective-permute-done | bytes 131104 | tf_op jit(solution)/shard_map/ppermute | solution.py:21
  23.0 0.5 fusion.26
  23.8 0.9 copy-done
  27.6 1.0 fusion.15
  28.6 1.0 convolution_dynamic-update-slice_fusion.8
  29.5 0.9 convolution_dynamic-update-slice_fusion.7
  30.5 0.9 convolution_dynamic-update-slice_fusion.6
  31.4 0.9 convolution_dynamic-update-slice_fusion.5
  32.4 1.0 convolution_dynamic-update-slice_fusion.4
  33.3 0.9 convolution_dynamic-update-slice_fusion.3
  34.3 1.0 convolution_dynamic-update-slice_fusion.2
  35.2 1.3 collective-permute-start.3
  36.5 1.0 convolution_dynamic-update-slice_fusion.1
  37.5 1.9 %collective-permute-done.3 = bf16[2,2,128,128]{3,2,1,0:T(8,128)(2,1)S(1)} collective-permute-done((bf16[2,2,128,128]{3,2,1,0:T(8,128)(2,1)S(1)}, bf16[2,2,128,128]{3,2,1,0:T(8,128)(2,1)S(1)}, u32[]{:S(2)}, u32[]{:S(2)}) %collective-permute-start.3) | collective-permute-done | bytes 131104 | tf_op jit(solution)/shard_map/ppermute | solution.py:10
  39.4 4.3 %collective-permute-start.4 = (bf16[4,1,128,128]{3,2,1,0:T(8,128)(2,1)S(1)}, bf16[4,1,128,128]{3,2,1,0:T(8,128)(2,1)S(1)}, u32[]{:S(2)}, u32[]{:S(2)}) collective-permute-start(bf16[4,1,128,128]{3,2,1,0:T(8,128)(2,1)S(1)} %get-tuple-element.51), channel_id=1, source_target_pairs={{0,1},{1,2},{2,3},{3,4},{4,5},{5,6},{6,7},{8,9},{9,10},{10,11},{11... | collective-permute-start | bytes 393224 | tf_op jit(solution)/shard_map/ppermute | solution.py:18
  43.7 1.3 collective-permute-start.5
  45.0 1.0 convolution_dynamic-update-slice_fusion
  46.2 4.4 %collective-permute-done.5 = bf16[4,1,128,128]{3,2,1,0:T(8,128)(2,1)S(1)} collective-permute-done((bf16[4,1,128,128]{3,2,1,0:T(8,128)(2,1)S(1)}, bf16[4,1,128,128]{3,2,1,0:T(8,128)(2,1)S(1)}, u32[]{:S(2)}, u32[]{:S(2)}) %collective-permute-start.5) | collective-permute-done | bytes 131104 | tf_op jit(solution)/shard_map/ppermute | solution.py:21
  50.9 0.5 fusion.25
  52.2 0.3 convolution_add_fusion.7
  53.8 64.0 %reduce-scatter.5.cloned.1.call-done = f32[16,3456]{1,0:T(8,128)} async-done(((f32[128,3456]{1,0:T(8,128)}), f32[16,3456]{1,0:T(8,128)}) %reduce-scatter.5.cloned.1.call-update) | async-done | bytes 221200 | tf_op jit(solution)/shard_map/reduce_scatter | solution.py:80
  117.8 2.7 %copy.8 = f32[16,3456]{0,1:T(8,128)} copy(f32[16,3456]{1,0:T(8,128)} %reduce-scatter.5.cloned.1.call-done) | data formatting | bytes 442368
  120.6 0.3 convolution_add_fusion.1
  120.8 0.9 fusion
  121.8 27.1 %reduce-scatter.7.cloned.1.call-done = f32[864,16]{1,0:T(8,128)} async-done(((f32[3456,16]{1,0:T(8,128)}), f32[864,16]{1,0:T(8,128)}) %reduce-scatter.7.cloned.1.call-update) | async-done | bytes 55312
  148.9 1.8 %copy.9 = f32[16,864]{1,0:T(8,128)} copy(f32[16,864]{0,1:T(8,128)} %bitcast.172) | data formatting | bytes 110592
  (46 shorter events, 5.8 us)
Async XLA Ops:
  7.2 110.7 %reduce-scatter.5.cloned.1.call-start = ((), (), s32[]{:S(2)}) async-start(), calls=%async_computation.2 | async-start | bytes 1990656 | tf_op jit(solution)/shard_map/reduce_scatter | solution.py:80
  7.2 3.5 %collective-permute-start = (bf16[2,2,128,128]{3,2,1,0:T(8,128)(2,1)}, bf16[2,2,128,128]{3,2,1,0:T(8,128)(2,1)S(1)}, u32[]{:S(2)}, u32[]{:S(2)}) collective-permute-start(bf16[2,2,128,128]{3,2,1,0:T(8,128)(2,1)} %param.3), channel_id=1, source_target_pairs={{0,8},{8,16},{16,24},{1,9},{9,17},{17,25},{2,10},{10,18},{18,26},{... | collective-permute-start | bytes 393224 | tf_op jit(solution)/shard_map/ppermute | solution.py:10
  11.7 7.6 %collective-permute-start.1 = (bf16[4,1,128,128]{3,2,1,0:T(8,128)(2,1)S(1)}, bf16[4,1,128,128]{3,2,1,0:T(8,128)(2,1)S(1)}, u32[]{:S(2)}, u32[]{:S(2)}) collective-permute-start(bf16[4,1,128,128]{3,2,1,0:T(8,128)(2,1)S(1)} %get-tuple-element.60), channel_id=1, source_target_pairs={{0,1},{1,2},{2,3},{3,4},{4,5},{5,6},{6,7},{8,9},{9,10},{10,11},{11... | collective-permute-start | bytes 393224 | tf_op jit(solution)/shard_map/ppermute | solution.py:18
  16.0 6.9 %collective-permute-start.2 = (bf16[4,1,128,128]{3,2,1,0:T(8,128)(2,1)S(1)}, bf16[4,1,128,128]{3,2,1,0:T(8,128)(2,1)S(1)}, u32[]{:S(2)}, u32[]{:S(2)}) collective-permute-start(bf16[4,1,128,128]{3,2,1,0:T(8,128)(2,1)S(1)} %get-tuple-element.61), channel_id=1, source_target_pairs={{1,0},{2,1},{3,2},{4,3},{5,4},{6,5},{7,6},{9,8},{10,9},{11,10},{12... | collective-permute-start | bytes 393224 | tf_op jit(solution)/shard_map/ppermute | solution.py:21
  23.5 1.2 copy-start
  25.6 0.9 copy-start.1
  26.6 0.9 copy-start.2
  35.2 4.1 %collective-permute-start.3 = (bf16[2,2,128,128]{3,2,1,0:T(8,128)(2,1)S(1)}, bf16[2,2,128,128]{3,2,1,0:T(8,128)(2,1)S(1)}, u32[]{:S(2)}, u32[]{:S(2)}) collective-permute-start(bf16[2,2,128,128]{3,2,1,0:T(8,128)(2,1)S(1)} %bitcast.122), channel_id=1, source_target_pairs={{8,0},{16,8},{24,16},{9,1},{17,9},{25,17},{10,2},{18,10},{26,18},{... | collective-permute-start | bytes 393224 | tf_op jit(solution)/shard_map/ppermute | solution.py:10
  39.4 6.8 %collective-permute-start.4 = (bf16[4,1,128,128]{3,2,1,0:T(8,128)(2,1)S(1)}, bf16[4,1,128,128]{3,2,1,0:T(8,128)(2,1)S(1)}, u32[]{:S(2)}, u32[]{:S(2)}) collective-permute-start(bf16[4,1,128,128]{3,2,1,0:T(8,128)(2,1)S(1)} %get-tuple-element.51), channel_id=1, source_target_pairs={{0,1},{1,2},{2,3},{3,4},{4,5},{5,6},{6,7},{8,9},{9,10},{10,11},{11... | collective-permute-start | bytes 393224 | tf_op jit(solution)/shard_map/ppermute | solution.py:18
  43.7 6.9 %collective-permute-start.5 = (bf16[4,1,128,128]{3,2,1,0:T(8,128)(2,1)S(1)}, bf16[4,1,128,128]{3,2,1,0:T(8,128)(2,1)S(1)}, u32[]{:S(2)}, u32[]{:S(2)}) collective-permute-start(bf16[4,1,128,128]{3,2,1,0:T(8,128)(2,1)S(1)} %get-tuple-element.52), channel_id=1, source_target_pairs={{1,0},{2,1},{3,2},{4,3},{5,4},{6,5},{7,6},{9,8},{10,9},{11,10},{12... | collective-permute-start | bytes 393224 | tf_op jit(solution)/shard_map/ppermute | solution.py:21
  46.0 102.9 %reduce-scatter.7.cloned.1.call-start = ((), (), s32[]{:S(2)}) async-start(), calls=%async_computation.3 | async-start | bytes 2211840
Sparse Core Ops, SparseCore 0:
  46.2 71.6 reduce-scatter.4
  120.7 28.1 reduce-scatter.6
where the time goes:
time: 158 us
  waiting for transfers between devices  102 us (65%)
  starting transfers between devices  14.9 us (9%)
  matrix products  14.7 us (9%)
  between operations  14.4 us (9%)
  local copies, waits for them, and re-layouts  9.93 us (6%)
    reduce_scatter x1, waiting for transfers between devices, local(): lax.psum_scatter(partial_grad, 'rows', scatter_dimension=0, tiled=True)  64 us
    unnamed x3, waiting for transfers between devices  27.2 us
    dot_general x9, matrix products, local(): lax.dot_general(pre_grad, piece, (((0,), (0,)), ((), ())), preferred_elem...  8.64 us
    ppermute x2, starting transfers between devices, padded(): lax.ppermute(lax.slice_in_dim(block, block.shape[dim] - width, None, axis...  8.59 us
    ppermute x2, waiting for transfers between devices, padded(): lax.ppermute(lax.slice_in_dim(block, 0, width, axis=dim), axis, backward)  7.84 us
    unnamed x10, local copies, waits for them, and re-layouts  7.8 us
    dot_general x16, matrix products, apply_taps(): jnp.dot(patches[index], kmat[index // 3, index % 3], preferred_element_ty...  5.59 us
    ppermute x2, starting transfers between devices, passed_along(): return lax.ppermute(x, axis, pairs)  3.65 us
  transfers between devices with their start and end apart: 8, of which 7 were waited for; matrix products, arithmetic and copies ran while one was open for 5% of the time, Pallas kernels for 0%

commit v1 on v0

v1 whole, which is shorter than its diff:
```python
import functools

import jax
import jax.numpy as jnp
from jax import lax
from jax.experimental import pallas as pl
from jax.experimental.pallas import tpu as pltpu
from jax.sharding import PartitionSpec as P

MESH = pl.DeviceIdType.MESH
F32 = jnp.float32
BF16 = jnp.bfloat16


def along_width(lines, width):
    count, _, chans = lines.shape
    flat = lines.reshape(count * width, chans).astype(F32)
    column = lax.broadcasted_iota(jnp.int32, (count, width, chans), 1).reshape(flat.shape)
    before = jnp.where(column == 0, 0.0, pltpu.roll(flat, 1, 0)).astype(BF16)
    after = jnp.where(column == width - 1, 0.0, pltpu.roll(flat, count * width - 1, 0)).astype(BF16)
    return (
        before.reshape(lines.shape),
        lines,
        after.reshape(lines.shape),
    )


def kernel(
    nt, nr, reduce_here,
    video, weights, cot, act, igrad, kgrad,
    taps, seen, patches, gext, gpatches, total, chunks,
    s0, r0, a1, s1a, r1a, s1b, r1b, a2a, a2b, s2a, r2a, s2b, r2b, a3, s3, r3,
    local_sem, vsend, vrecv, gsend, grecv, ksend, krecv,
):
    frames, height, width, chans = video.shape
    rows = frames * height * width
    tm = lax.axis_index("tm")
    row = lax.axis_index("rows")

    def inside(dt, dr):
        return (tm + dt >= 0) & (tm + dt < nt) & (row + dr >= 0) & (row + dr < nr)

    def wrapped(dt, dr):
        return (lax.rem(tm + dt + nt, nt), lax.rem(row + dr + nr, nr))

    load = pltpu.make_async_copy(weights, taps, local_sem)
    load.start()

    barrier = pltpu.get_barrier_semaphore()
    around = [(dt, dr) for dt in (-1, 0, 1) for dr in (-1, 0, 1) if dt or dr]
    expected = 0
    for dt, dr in around:
        there = inside(dt, dr)
        expected = expected + jnp.where(there, 1, 0)

        @pl.when(there)
        def _(dt=dt, dr=dr):
            pl.semaphore_signal(barrier, inc=1, device_id=wrapped(dt, dr), device_id_type=MESH)

    if reduce_here:
        depth = lax.div(row, 2)
        side = lax.rem(row, 2)
        across = lax.div(tm, 2)
        core = lax.rem(tm, 2)
        other_core = (across * 2 + 1 - core, row)
        other_across = ((1 - across) * 2 + core, row)
        other_side = (tm, depth * 2 + 1 - side)
        layers = [lax.rem(depth + k, 4) for k in range(4)]
        partners = [other_across] + [(tm, layers[k] * 2 + side) for k in (1, 2, 3)]
        for partner in partners:
            pl.semaphore_signal(barrier, inc=1, device_id=partner, device_id_type=MESH)
        expected = expected + len(partners)
    pl.semaphore_wait(barrier, expected)

    def exchange(pieces, send_sems, recv_sems):
        copies = []
        for k, (dt, dr, source, target) in enumerate(pieces):
            copy = pltpu.make_async_remote_copy(
                src_ref=source, dst_ref=target,
                send_sem=send_sems.at[k], recv_sem=recv_sems.at[k],
                device_id=wrapped(dt, dr), device_id_type=MESH,
            )
            copies.append(copy)
            pl.when(inside(dt, dr))(copy.start)

        def arrive(k):
            dt, dr, _, target = pieces[k]
            there = inside(-dt, -dr)
            pl.when(there)(copies[k].wait_recv)

            @pl.when(jnp.logical_not(there))
            def _():
                target[...] = jnp.zeros(target.shape, BF16)

        def finish():
            for k, (dt, dr, _, _) in enumerate(pieces):
                pl.when(inside(dt, dr))(copies[k].wait_send)

        return arrive, finish

    own, top, bottom = pl.ds(1, height), 0, height + 1
    old, new = pl.ds(0, 2), pl.ds(2, frames)
    last = pl.ds(frames - 2, 2)
    arrive_v, finish_v = exchange(
        [
            (1, 0, video.at[last], seen.at[old, own]),
            (0, 1, video.at[:, height - 1], seen.at[new, top]),
            (0, -1, video.at[:, 0], seen.at[new, bottom]),
            (1, 1, video.at[last, height - 1], seen.at[old, top]),
            (1, -1, video.at[last, 0], seen.at[old, bottom]),
        ],
        vsend, vrecv,
    )

    def spread(target, fr, ro, lines):
        flat = lines.reshape((-1,) + lines.shape[-2:])
        for c, piece in enumerate(along_width(flat, width)):
            target[fr, ro, :, c * chans:(c + 1) * chans] = piece.reshape(lines.shape)

    def patch(source, a, b):
        return source[a:a + frames, b:b + height].reshape(rows, 3 * chans)

    def forward(a, b):
        return jnp.dot(patch(patches, a, b), taps[a * 3 + b], preferred_element_type=F32)

    spread(patches, new, own, video[...])
    load.wait()
    pre = forward(2, 1)
    arrive_v(0)
    spread(patches, old, own, seen[old, own])
    pre = pre + forward(0, 1)
    pre = pre + forward(1, 1)
    for k, fr, ro in ((1, new, top), (2, new, bottom), (3, old, top), (4, old, bottom)):
        arrive_v(k)
        spread(patches, fr, ro, seen[fr, ro])
    for b in (0, 2):
        for a in range(3):
            pre = pre + forward(a, b)

    sig = 1.0 / (1.0 + jnp.exp(-pre))
    act[...] = (pre * sig).astype(BF16).reshape(act.shape)
    cot_flat = cot[...].reshape(rows, chans).astype(F32)
    grad = (cot_flat * sig * (1.0 + pre * (1.0 - sig))).astype(BF16)
    mine, later = pl.ds(0, frames), pl.ds(frames, 2)
    early = pl.ds(0, 2)
    gext[mine, own] = grad.reshape(video.shape)
    arrive_g, finish_g = exchange(
        [
            (-1, 0, gext.at[early, own], gext.at[later, own]),
            (0, 1, gext.at[mine, height], gext.at[mine, top]),
            (0, -1, gext.at[mine, 1], gext.at[mine, bottom]),
            (-1, 1, gext.at[early, height], gext.at[later, top]),
            (-1, -1, gext.at[early, 1], gext.at[later, bottom]),
        ],
        gsend, grecv,
    )

    turned = grad.astype(F32).T.astype(BF16)
    kdepth = 3 * chans

    def weight_part(k):
        total[:, k * kdepth:(k + 1) * kdepth] = jnp.dot(
            turned, patch(patches, k // 3, k % 3), preferred_element_type=F32
        )

    def backward(a, b):
        block = taps.at[(2 - a) * 3 + 2 - b]
        mat = jnp.concatenate(
            [block[(2 - c) * chans:(3 - c) * chans, :] for c in range(3)], axis=1
        )
        return lax.dot_general(
            patch(gpatches, a, b), mat, (((1,), (1,)), ((), ())), preferred_element_type=F32
        )

    def grad_own():
        spread(gpatches, mine, own, grad.reshape(video.shape))
        return backward(0, 1)

    def grad_later(out):
        arrive_g(0)
        spread(gpatches, later, own, gext[later, own])
        return out + backward(1, 1) + backward(2, 1)

    def grad_edges():
        for k, fr, ro in ((1, mine, top), (2, mine, bottom), (3, later, top), (4, later, bottom)):
            arrive_g(k)
            spread(gpatches, fr, ro, gext[fr, ro])

    if not reduce_here:
        for k in range(9):
            weight_part(k)
        kgrad[...] = total[...]
        out = grad_later(grad_own())
        grad_edges()
        for b in (0, 2):
            for a in range(3):
                out = out + backward(a, b)
        igrad[...] = out.astype(BF16).reshape(igrad.shape)
        finish_v()
        finish_g()
        return

    columns = total.shape[1] // nt
    wide = chunks.shape[-1]

    def cut(j):
        start = columns * j // 128 * 128
        shift = columns * j - start
        span = -(-(shift + columns) // 128) * 128
        piece = total[:, start:start + span]
        if shift:
            piece = pltpu.roll(piece, span - shift, 1)
        chunks[j] = piece[:, :wide].reshape(chunks.shape[1:])

    def send(k, source, target, device):
        copy = pltpu.make_async_remote_copy(
            src_ref=source, dst_ref=target,
            send_sem=ksend.at[k], recv_sem=krecv.at[k],
            device_id=device, device_id_type=MESH,
        )
        copy.start()
        return copy

    copies = []
    done = 0
    for half in range(2):
        need = -(-columns * (2 * half + 2) // kdepth)
        for k in range(done, need):
            weight_part(k)
        done = need
        cut(2 * half)
        cut(2 * half + 1)
        s0[half] = chunks[2 * half + 1 - core].astype(BF16)
        copies.append(send(half, s0.at[half], r0.at[half], other_core))

    out = grad_own()

    for half in range(2):
        copies[half].wait_recv()
        a1[half] = chunks[2 * half + core] + r0[half].astype(F32)
    s1a[...] = a1[1 - across, 0:2].astype(BF16)
    copies.append(send(2, s1a, r1a, other_across))
    s1b[...] = a1[:, 2:4, 1 - side].astype(BF16)
    copies.append(send(3, s1b, r1b, other_side))

    out = grad_later(out)
    grad_edges()

    copies[2].wait_recv()
    a2a[...] = a1[across, 0:2] + r1a[...].astype(F32)
    s2a[...] = a2a[:, 1 - side].astype(BF16)
    copies.append(send(4, s2a, r2a, other_side))
    copies[3].wait_recv()
    a2b[...] = a1[:, 2:4, side] + r1b[...].astype(F32)
    s2b[...] = a2b[1 - across].astype(BF16)
    copies.append(send(5, s2b, r2b, other_across))

    for a in range(3):
        out = out + backward(a, 0)

    copies[4].wait_recv()
    a3[0:2] = a2a[:, side] + r2a[...].astype(F32)
    copies[5].wait_recv()
    a3[2:4] = a2b[across] + r2b[...].astype(F32)
    for k in (1, 2, 3):
        s3[k - 1] = a3[layers[k]].astype(BF16)
        copies.append(
            send(5 + k, s3.at[k - 1], r3.at[k - 1], (tm, layers[k] * 2 + side))
        )

    for a in range(3):
        out = out + backward(a, 2)
    igrad[...] = out.astype(BF16).reshape(igrad.shape)

    owned = a3[depth]
    for k in (1, 2, 3):
        copies[5 + k].wait_recv()
        owned = owned + r3[k - 1].astype(F32)
    kgrad[...] = owned[:, :columns]
    for copy in copies:
        copy.wait_send()
    finish_v()
    finish_g()


def local(nt, nr, video, weights, cotangent):
    frames, height, width, chans = video.shape
    rows = frames * height * width
    cols = 27 * chans
    share, columns = chans // nr, cols // nt
    reduce_here = nt == 4 and nr == 8 and share % 16 == 0
    wide = -(-columns // 128) * 128 if reduce_here else 128
    sh = share if reduce_here else 16
    vm = pltpu.VMEM
    full = pl.BlockSpec(memory_space=pltpu.VMEM)
    scratch = [
        vm((9, 3 * chans, chans), BF16),
        vm((frames + 2, height + 2, width, chans), BF16),
        vm((frames + 2, height + 2, width, 3 * chans), BF16),
        vm((frames + 2, height + 2, width, chans), BF16),
        vm((frames + 2, height + 2, width, 3 * chans), BF16),
        vm((chans, cols), F32),
        vm((4, 4, 2, sh, wide), F32),
        vm((2, 4, 2, sh, wide), BF16),
        vm((2, 4, 2, sh, wide), BF16),
        vm((2, 4, 2, sh, wide), F32),
        vm((2, 2, sh, wide), BF16),
        vm((2, 2, sh, wide), BF16),
        vm((2, 2, sh, wide), BF16),
        vm((2, 2, sh, wide), BF16),
        vm((2, 2, sh, wide), F32),
        vm((2, 2, sh, wide), F32),
        vm((2, sh, wide), BF16),
        vm((2, sh, wide), BF16),
        vm((2, sh, wide), BF16),
        vm((2, sh, wide), BF16),
        vm((4, sh, wide), F32),
        vm((3, sh, wide), BF16),
        vm((3, sh, wide), BF16),
        pltpu.SemaphoreType.DMA,
        pltpu.SemaphoreType.DMA((5,)),
        pltpu.SemaphoreType.DMA((5,)),
        pltpu.SemaphoreType.DMA((5,)),
        pltpu.SemaphoreType.DMA((5,)),
        pltpu.SemaphoreType.DMA((9,)),
        pltpu.SemaphoreType.DMA((9,)),
    ]
    kshape = (share, columns) if reduce_here else (chans, cols)
    activated, input_grad, kgrad = pl.pallas_call(
        functools.partial(kernel, nt, nr, reduce_here),
        out_shape=(
            jax.ShapeDtypeStruct(video.shape, BF16),
            jax.ShapeDtypeStruct(video.shape, BF16),
            jax.ShapeDtypeStruct(kshape, F32),
        ),
        in_specs=[full, pl.BlockSpec(memory_space=pl.ANY), full],
        out_specs=(full, full, full),
        scratch_shapes=scratch,
        compiler_params=pltpu.CompilerParams(
            collective_id=0, has_side_effects=True, vmem_limit_bytes=40 * 1024 * 1024
        ),
        cost_estimate=pl.CostEstimate(
            flops=6 * rows * cols * chans, bytes_accessed=4 * 1024 * 1024, transcendentals=rows * chans
        ),
        name="conv_silu_grads",
    )(video, weights.reshape(9, 3 * chans, chans), cotangent)
    if not reduce_here:
        kgrad = lax.psum_scatter(kgrad, "rows", scatter_dimension=0, tiled=True)
        kgrad = lax.psum_scatter(kgrad, "tm", scatter_dimension=1, tiled=True)
    return activated, input_grad, kgrad


def solution(mesh):
    split = P("tm", "rows", None, None)
    return jax.shard_map(
        functools.partial(local, mesh.shape["tm"], mesh.shape["rows"]),
        mesh=mesh,
        in_specs=(split, P(), split),
        out_specs=(split, split, P("rows", "tm")),
        check_vma=False,
    )
```

time: 158 us -> 34.1 us (0.22)
  waiting for transfers between devices: 102 us -> 0 us
  Pallas kernels: 0 us -> 28.3 us
  starting transfers between devices: 14.9 us -> 0 us
  matrix products: 14.7 us -> 0 us
  between operations: 14.4 us -> 0.65 us
  local copies, waits for them, and re-layouts: 9.93 us -> 4.9 us
    reduce_scatter x1 -> x0, waiting for transfers between devices: 64 us -> none  [local(): lax.psum_scatter(partial_grad, 'rows', scatter_dimension=0, tiled=True)]
    pallas_call x0 -> x1, Pallas kernels: none -> 28.3 us  [local(): pl.pallas_call(functools.partial(kernel, nt, nr, reduce_here), out_shape=...]
    unnamed x3 -> x0, waiting for transfers between devices: 27.2 us -> none
    ppermute x6 -> x0, starting transfers between devices: 14.8 us -> none  [the longest x2 8.59 us: padded(): lax.ppermute(lax.slice_in_dim(block, block.shape[dim] - width, None, axis...]
    dot_general x27 -> x0, matrix products: 14.7 us -> none  [the longest x9 8.64 us: local(): lax.dot_general(pre_grad, piece, (((0,), (0,)), ((), ())), preferred_elem...]
    ppermute x6 -> x0, waiting for transfers between devices: 11 us -> none  [the longest x2 7.84 us: padded(): lax.ppermute(lax.slice_in_dim(block, 0, width, axis=dim), axis, backward)]
    unnamed x10 -> x9, local copies, waits for them, and re-layouts: 7.8 us -> 4.9 us
  transfers between devices with their start and end apart: 8 -> 0, of which waited for: 7 -> 0; matrix products, arithmetic and copies ran while one was open for 5% -> 0% of each run, Pallas kernels for 0% -> 0%
where the time goes in v1:
time: 34.1 us; the launch traced here: 33.9 us
  Pallas kernels  28.3 us (83%)
  local copies, waits for them, and re-layouts  4.9 us (14%)
  between operations  0.65 us (2%)
    pallas_call x1, Pallas kernels, local(): pl.pallas_call(functools.partial(kernel, nt, nr, reduce_here), out_shape=...  28.3 us
    unnamed x9, local copies, waits for them, and re-layouts  4.9 us

profile of v1, /device:TPU:0, one launch (start us, length us, event | category | flops | bytes accessed | tf_op | source)
XLA Modules:
  0.0 33.9 jit_solution(8769825334982318573)
XLA Ops:
  0.6 0.0 copy-start
  0.6 1.2 %copy-done = bf16[3,3,3,128,128]{4,3,2,1,0:T(8,128)(2,1)S(1)} copy-done((bf16[3,3,3,128,128]{4,3,2,1,0:T(8,128)(2,1)S(1)}, bf16[3,3,3,128,128]{4,3,2,1,0:T(8,128)(2,1)}, u32[]{:S(2)}) %copy-start) | copy-done | bytes 884760
  1.8 0.0 copy-start.1
  1.8 0.9 %copy-done.1 = bf16[2,2,128,128]{3,2,1,0:T(8,128)(2,1)S(1)} copy-done((bf16[2,2,128,128]{3,2,1,0:T(8,128)(2,1)S(1)}, bf16[2,2,128,128]{3,2,1,0:T(8,128)(2,1)}, u32[]{:S(2)}) %copy-start.1) | copy-done | bytes 131096
  2.7 0.0 copy-start.2
  2.7 0.9 %copy-done.2 = bf16[2,2,128,128]{3,2,1,0:T(8,128)(2,1)S(1)} copy-done((bf16[2,2,128,128]{3,2,1,0:T(8,128)(2,1)S(1)}, bf16[2,2,128,128]{3,2,1,0:T(8,128)(2,1)}, u32[]{:S(2)}) %copy-start.2) | copy-done | bytes 131096
  3.6 28.3 %conv_silu_grads.1 = (bf16[2,2,128,128]{3,2,1,0:T(8,128)(2,1)S(1)}, bf16[2,2,128,128]{3,2,1,0:T(8,128)(2,1)S(1)}, f32[16,864]{1,0:T(8,128)S(1)}) custom-call(bf16[2,2,128,128]{3,2,1,0:T(8,128)(2,1)S(1)} %copy-done.1, bf16[9,384,128]{2,1,0:T(8,128)(2,1)S(1)} %bitcast.1, bf16[2,2,128,128]{3,2,1,0:T(8,128)(2,1)S(1)} %copy-done.2), custom_call_target="tpu_custom_call" | custom-call | flops 1358954496 | bytes 4194304 | tf_op jit(solution)/shard_map/conv_silu_grads/pallas_call | solution.py:329
  32.0 0.7 %copy.9 = bf16[2,2,128,128]{3,2,1,0:T(8,128)(2,1)} copy(bf16[2,2,128,128]{3,2,1,0:T(8,128)(2,1)S(1)} %get-tuple-element.6) | data formatting | bytes 262144
  32.6 0.7 %copy.10 = bf16[2,2,128,128]{3,2,1,0:T(8,128)(2,1)} copy(bf16[2,2,128,128]{3,2,1,0:T(8,128)(2,1)S(1)} %get-tuple-element.7) | data formatting | bytes 262144
  33.3 0.6 %copy.11 = f32[16,864]{1,0:T(8,128)} copy(f32[16,864]{1,0:T(8,128)S(1)} %get-tuple-element.8) | data formatting | bytes 110592
Async XLA Ops:
  0.6 1.2 %copy-start = (bf16[3,3,3,128,128]{4,3,2,1,0:T(8,128)(2,1)S(1)}, bf16[3,3,3,128,128]{4,3,2,1,0:T(8,128)(2,1)}, u32[]{:S(2)}) copy-start(bf16[3,3,3,128,128]{4,3,2,1,0:T(8,128)(2,1)} %param.4) | copy-start | bytes 2654212
  1.8 0.9 %copy-start.1 = (bf16[2,2,128,128]{3,2,1,0:T(8,128)(2,1)S(1)}, bf16[2,2,128,128]{3,2,1,0:T(8,128)(2,1)}, u32[]{:S(2)}) copy-start(bf16[2,2,128,128]{3,2,1,0:T(8,128)(2,1)} %video.1) | copy-start | bytes 393220
  2.7 0.9 %copy-start.2 = (bf16[2,2,128,128]{3,2,1,0:T(8,128)(2,1)S(1)}, bf16[2,2,128,128]{3,2,1,0:T(8,128)(2,1)}, u32[]{:S(2)}) copy-start(bf16[2,2,128,128]{3,2,1,0:T(8,128)(2,1)} %cot.1) | copy-start | bytes 393220

commit v2 on v1

--- a/solution.py
+++ b/solution.py
@@ -10,6 +10,7 @@
 MESH = pl.DeviceIdType.MESH
 F32 = jnp.float32
 BF16 = jnp.bfloat16
+VMEM_BYTES = 56 * 1024 * 1024
 
 
 def along_width(lines, width):
@@ -27,8 +28,8 @@
 
 def kernel(
     nt, nr, reduce_here,
-    video, weights, cot, act, igrad, kgrad,
-    taps, seen, patches, gext, gpatches, total, chunks,
+    video, weights, cot, act_out, igrad_out, kgrad_out,
+    act, igrad, kgrad, taps, cot_own, seen, patches, gext, gpatches, total, chunks,
     s0, r0, a1, s1a, r1a, s1b, r1b, a2a, a2b, s2a, r2a, s2b, r2b, a3, s3, r3,
     local_sem, vsend, vrecv, gsend, grecv, ksend, krecv,
 ):
@@ -43,17 +44,28 @@
     def wrapped(dt, dr):
         return (lax.rem(tm + dt + nt, nt), lax.rem(row + dr + nr, nr))
 
-    load = pltpu.make_async_copy(weights, taps, local_sem)
-    load.start()
+    own, top, bottom = pl.ds(1, height), 0, height + 1
+    old, new = pl.ds(0, 2), pl.ds(2, frames)
+    loads = [
+        pltpu.make_async_copy(video, seen.at[new, own], local_sem.at[0]),
+        pltpu.make_async_copy(weights, taps, local_sem.at[1]),
+        pltpu.make_async_copy(cot, cot_own, local_sem.at[2]),
+    ]
+    for load in loads:
+        load.start()
 
     barrier = pltpu.get_barrier_semaphore()
+    odd = lax.rem(tm, 2) == 1
     around = [(dt, dr) for dt in (-1, 0, 1) for dr in (-1, 0, 1) if dt or dr]
     expected = 0
     for dt, dr in around:
-        there = inside(dt, dr)
-        expected = expected + jnp.where(there, 1, 0)
-
-        @pl.when(there)
+        greets = copies_to = inside(dt, dr)
+        if dt and dr:
+            greets = greets & (dt == -1) & jnp.logical_not(odd)
+            copies_to = copies_to & (dt == 1) & odd
+        expected = expected + jnp.where(copies_to, 1, 0)
+
+        @pl.when(greets)
         def _(dt=dt, dr=dr):
             pl.semaphore_signal(barrier, inc=1, device_id=wrapped(dt, dr), device_id_type=MESH)
 
@@ -72,45 +84,45 @@
         expected = expected + len(partners)
     pl.semaphore_wait(barrier, expected)
 
-    def exchange(pieces, send_sems, recv_sems):
-        copies = []
-        for k, (dt, dr, source, target) in enumerate(pieces):
-            copy = pltpu.make_async_remote_copy(
-                src_ref=source, dst_ref=target,
-                send_sem=send_sems.at[k], recv_sem=recv_sems.at[k],
-                device_id=wrapped(dt, dr), device_id_type=MESH,
-            )
-            copies.append(copy)
-            pl.when(inside(dt, dr))(copy.start)
-
-        def arrive(k):
-            dt, dr, _, target = pieces[k]
-            there = inside(-dt, -dr)
-            pl.when(there)(copies[k].wait_recv)
-
-            @pl.when(jnp.logical_not(there))
-            def _():
-                target[...] = jnp.zeros(target.shape, BF16)
-
-        def finish():
-            for k, (dt, dr, _, _) in enumerate(pieces):
-                pl.when(inside(dt, dr))(copies[k].wait_send)
-
-        return arrive, finish
-
-    own, top, bottom = pl.ds(1, height), 0, height + 1
-    old, new = pl.ds(0, 2), pl.ds(2, frames)
+    def piece(dt, dr, send_when, source, target, sems, k):
+        copy = pltpu.make_async_remote_copy(
+            src_ref=source, dst_ref=target,
+            send_sem=sems[0].at[k], recv_sem=sems[1].at[k],
+            device_id=wrapped(dt, dr), device_id_type=MESH,
+        )
+        return (copy, send_when)
+
+    def start(part):
+        pl.when(part[1])(part[0].start)
+
+    def sent(part):
+        pl.when(part[1])(part[0].wait_send)
+
+    def arrive(part, dt, dr, target):
+        there = inside(dt, dr)
+        pl.when(there)(part[0].wait_recv)
+
+        @pl.when(jnp.logical_not(there))
+        def _():
+            target[...] = jnp.zeros(target.shape, BF16)
+
     last = pl.ds(frames - 2, 2)
-    arrive_v, finish_v = exchange(
-        [
-            (1, 0, video.at[last], seen.at[old, own]),
-            (0, 1, video.at[:, height - 1], seen.at[new, top]),
-            (0, -1, video.at[:, 0], seen.at[new, bottom]),
-            (1, 1, video.at[last, height - 1], seen.at[old, top]),
-            (1, -1, video.at[last, 0], seen.at[old, bottom]),
-        ],
-        vsend, vrecv,
-    )
+    vsems, gsems = (vsend, vrecv), (gsend, grecv)
+    halo = [
+        piece(1, 0, inside(1, 0), video.at[last], seen.at[old, own], vsems, 0),
+        piece(0, 1, inside(0, 1), video.at[:, height - 1], seen.at[new, top], vsems, 1),
+        piece(0, -1, inside(0, -1), video.at[:, 0], seen.at[new, bottom], vsems, 2),
+        piece(1, 1, inside(1, 1) & odd, video.at[last, height - 1], seen.at[old, top], vsems, 3),
+        piece(1, -1, inside(1, -1) & odd, video.at[last, 0], seen.at[old, bottom], vsems, 4),
+    ]
+    for part in halo:
+        start(part)
+    even = jnp.logical_not(odd)
+    newest = pl.ds(frames, 2)
+    passed = [
+        piece(1, 0, inside(1, -1) & even, seen.at[newest, top], seen.at[old, top], vsems, 3),
+        piece(1, 0, inside(1, 1) & even, seen.at[newest, bottom], seen.at[old, bottom], vsems, 4),
+    ]
 
     def spread(target, fr, ro, lines):
         flat = lines.reshape((-1,) + lines.shape[-2:])
@@ -123,37 +135,53 @@
     def forward(a, b):
         return jnp.dot(patch(patches, a, b), taps[a * 3 + b], preferred_element_type=F32)
 
-    spread(patches, new, own, video[...])
-    load.wait()
+    loads[0].wait()
+    spread(patches, new, own, seen[new, own])
+    loads[1].wait()
     pre = forward(2, 1)
-    arrive_v(0)
+    arrive(halo[0], -1, 0, seen.at[old, own])
     spread(patches, old, own, seen[old, own])
     pre = pre + forward(0, 1)
     pre = pre + forward(1, 1)
-    for k, fr, ro in ((1, new, top), (2, new, bottom), (3, old, top), (4, old, bottom)):
-        arrive_v(k)
-        spread(patches, fr, ro, seen[fr, ro])
+    arrive(halo[1], 0, -1, seen.at[new, top])
+    start(passed[0])
+    arrive(halo[2], 0, 1, seen.at[new, bottom])
+    start(passed[1])
+    spread(patches, new, top, seen[new, top])
+    spread(patches, new, bottom, seen[new, bottom])
+    pre = pre + forward(2, 0)
+    pre = pre + forward(2, 2)
+    arrive(halo[3], -1, -1, seen.at[old, top])
+    spread(patches, old, top, seen[old, top])
+    arrive(halo[4], -1, 1, seen.at[old, bottom])
+    spread(patches, old, bottom, seen[old, bottom])
     for b in (0, 2):
-        for a in range(3):
+        for a in range(2):
             pre = pre + forward(a, b)
 
     sig = 1.0 / (1.0 + jnp.exp(-pre))
     act[...] = (pre * sig).astype(BF16).reshape(act.shape)
-    cot_flat = cot[...].reshape(rows, chans).astype(F32)
+    loads[2].wait()
+    stores = [
+        pltpu.make_async_copy(act, act_out, local_sem.at[3]),
+        pltpu.make_async_copy(igrad, igrad_out, local_sem.at[4]),
+        pltpu.make_async_copy(kgrad, kgrad_out, local_sem.at[5]),
+    ]
+    stores[0].start()
+    cot_flat = cot_own[...].reshape(rows, chans).astype(F32)
     grad = (cot_flat * sig * (1.0 + pre * (1.0 - sig))).astype(BF16)
     mine, later = pl.ds(0, frames), pl.ds(frames, 2)
     early = pl.ds(0, 2)
     gext[mine, own] = grad.reshape(video.shape)
-    arrive_g, finish_g = exchange(
-        [
-            (-1, 0, gext.at[early, own], gext.at[later, own]),
-            (0, 1, gext.at[mine, height], gext.at[mine, top]),
-            (0, -1, gext.at[mine, 1], gext.at[mine, bottom]),
-            (-1, 1, gext.at[early, height], gext.at[later, top]),
-            (-1, -1, gext.at[early, 1], gext.at[later, bottom]),
-        ],
-        gsend, grecv,
-    )
+    ghalo = [
+        piece(-1, 0, inside(-1, 0), gext.at[early, own], gext.at[later, own], gsems, 0),
+        piece(0, 1, inside(0, 1), gext.at[mine, height], gext.at[mine, top], gsems, 1),
+        piece(0, -1, inside(0, -1), gext.at[mine, 1], gext.at[mine, bottom], gsems, 2),
+        piece(-1, 0, inside(-1, -1), gext.at[early, top], gext.at[later, top], gsems, 3),
+        piece(-1, 0, inside(-1, 1), gext.at[early, bottom], gext.at[later, bottom], gsems, 4),
+    ]
+    for part in ghalo[:3]:
+        start(part)
 
     turned = grad.astype(F32).T.astype(BF16)
     kdepth = 3 * chans
@@ -177,27 +205,46 @@
         return backward(0, 1)
 
     def grad_later(out):
-        arrive_g(0)
+        arrive(ghalo[0], 1, 0, gext.at[later, own])
         spread(gpatches, later, own, gext[later, own])
         return out + backward(1, 1) + backward(2, 1)
 
-    def grad_edges():
-        for k, fr, ro in ((1, mine, top), (2, mine, bottom), (3, later, top), (4, later, bottom)):
-            arrive_g(k)
-            spread(gpatches, fr, ro, gext[fr, ro])
+    def grad_rows():
+        arrive(ghalo[1], 0, -1, gext.at[mine, top])
+        start(ghalo[3])
+        arrive(ghalo[2], 0, 1, gext.at[mine, bottom])
+        start(ghalo[4])
+
+    def grad_edges(out):
+        for ro in (top, bottom):
+            spread(gpatches, mine, ro, gext[mine, ro])
+        return out + backward(0, 0) + backward(0, 2)
+
+    def grad_corners(out):
+        arrive(ghalo[3], 1, -1, gext.at[later, top])
+        spread(gpatches, later, top, gext[later, top])
+        out = out + backward(1, 0) + backward(2, 0)
+        arrive(ghalo[4], 1, 1, gext.at[later, bottom])
+        spread(gpatches, later, bottom, gext[later, bottom])
+        out = out + backward(1, 2) + backward(2, 2)
+        igrad[...] = out.astype(BF16).reshape(igrad.shape)
+        stores[1].start()
+
+    def finish():
+        for part in halo + passed + ghalo:
+            sent(part)
+        for store in stores:
+            store.wait()
 
     if not reduce_here:
         for k in range(9):
             weight_part(k)
         kgrad[...] = total[...]
+        stores[2].start()
         out = grad_later(grad_own())
-        grad_edges()
-        for b in (0, 2):
-            for a in range(3):
-                out = out + backward(a, b)
-        igrad[...] = out.astype(BF16).reshape(igrad.shape)
-        finish_v()
-        finish_g()
+        grad_rows()
+        grad_corners(grad_edges(out))
+        finish()
         return
 
     columns = total.shape[1] // nt
@@ -244,7 +291,6 @@
     copies.append(send(3, s1b, r1b, other_side))
 
     out = grad_later(out)
-    grad_edges()
 
     copies[2].wait_recv()
     a2a[...] = a1[across, 0:2] + r1a[...].astype(F32)
@@ -255,8 +301,8 @@
     s2b[...] = a2b[1 - across].astype(BF16)
     copies.append(send(5, s2b, r2b, other_across))
 
-    for a in range(3):
-        out = out + backward(a, 0)
+    grad_rows()
+    out = grad_edges(out)
 
     copies[4].wait_recv()
     a3[0:2] = a2a[:, side] + r2a[...].astype(F32)
@@ -268,19 +314,26 @@
             send(5 + k, s3.at[k - 1], r3.at[k - 1], (tm, layers[k] * 2 + side))
         )
 
-    for a in range(3):
-        out = out + backward(a, 2)
-    igrad[...] = out.astype(BF16).reshape(igrad.shape)
+    grad_corners(out)
 
     owned = a3[depth]
     for k in (1, 2, 3):
         copies[5 + k].wait_recv()
         owned = owned + r3[k - 1].astype(F32)
     kgrad[...] = owned[:, :columns]
+    stores[2].start()
     for copy in copies:
         copy.wait_send()
-    finish_v()
-    finish_g()
+    finish()
+
+
+def deliver(*refs):
+    count = (len(refs) - 1) // 2
+    copies = [pltpu.make_async_copy(refs[k], refs[count + k], refs[-1].at[k]) for k in range(count)]
+    for copy in copies:
+        copy.start()
+    for copy in copies:
+        copy.wait()
 
 
 def local(nt, nr, video, weights, cotangent):
@@ -292,9 +345,14 @@
     wide = -(-columns // 128) * 128 if reduce_here else 128
     sh = share if reduce_here else 16
     vm = pltpu.VMEM
-    full = pl.BlockSpec(memory_space=pltpu.VMEM)
+    far = pl.BlockSpec(memory_space=pl.ANY)
+    kshape = (share, columns) if reduce_here else (chans, cols)
     scratch = [
+        vm(video.shape, BF16),
+        vm(video.shape, BF16),
+        vm(kshape, F32),
         vm((9, 3 * chans, chans), BF16),
+        vm(video.shape, BF16),
         vm((frames + 2, height + 2, width, chans), BF16),
         vm((frames + 2, height + 2, width, 3 * chans), BF16),
         vm((frames + 2, height + 2, width, chans), BF16),
@@ -317,7 +375,7 @@
         vm((4, sh, wide), F32),
         vm((3, sh, wide), BF16),
         vm((3, sh, wide), BF16),
-        pltpu.SemaphoreType.DMA,
+        pltpu.SemaphoreType.DMA((6,)),
         pltpu.SemaphoreType.DMA((5,)),
         pltpu.SemaphoreType.DMA((5,)),
         pltpu.SemaphoreType.DMA((5,)),
@@ -325,7 +383,6 @@
         pltpu.SemaphoreType.DMA((9,)),
         pltpu.SemaphoreType.DMA((9,)),
     ]
-    kshape = (share, columns) if reduce_here else (chans, cols)
     activated, input_grad, kgrad = pl.pallas_call(
         functools.partial(kernel, nt, nr, reduce_here),
         out_shape=(
@@ -333,11 +390,11 @@
             jax.ShapeDtypeStruct(video.shape, BF16),
             jax.ShapeDtypeStruct(kshape, F32),
         ),
-        in_specs=[full, pl.BlockSpec(memory_space=pl.ANY), full],
-        out_specs=(full, full, full),
+        in_specs=[far, far, far],
+        out_specs=(far, far, far),
         scratch_shapes=scratch,
         compiler_params=pltpu.CompilerParams(
-            collective_id=0, has_side_effects=True, vmem_limit_bytes=40 * 1024 * 1024
+            collective_id=0, has_side_effects=True, vmem_limit_bytes=VMEM_BYTES
         ),
         cost_estimate=pl.CostEstimate(
             flops=6 * rows * cols * chans, bytes_accessed=4 * 1024 * 1024, transcendentals=rows * chans
@@ -347,7 +404,17 @@
     if not reduce_here:
         kgrad = lax.psum_scatter(kgrad, "rows", scatter_dimension=0, tiled=True)
         kgrad = lax.psum_scatter(kgrad, "tm", scatter_dimension=1, tiled=True)
-    return activated, input_grad, kgrad
+        return activated, input_grad, kgrad
+    results = (activated, input_grad, kgrad)
+    return pl.pallas_call(
+        deliver,
+        out_shape=tuple(jax.ShapeDtypeStruct(x.shape, x.dtype) for x in results),
+        in_specs=[far] * 3,
+        out_specs=(far,) * 3,
+        scratch_shapes=[pltpu.SemaphoreType.DMA((3,))],
+        compiler_params=pltpu.CompilerParams(vmem_limit_bytes=VMEM_BYTES),
+        name="deliver",
+    )(*results)
 
 
 def solution(mesh):

time: 34.1 us -> 39.5 us (1.16)
  Pallas kernels: 28.3 us -> 38.7 us
  local copies, waits for them, and re-layouts: 4.9 us -> 0 us
    pallas_call x0 -> x1, Pallas kernels: none -> 10.8 us  [local(): pl.pallas_call(deliver, out_shape=tuple((jax.ShapeDtypeStruct(x.shape, x....]
    unnamed x9 -> x0, local copies, waits for them, and re-layouts: 4.9 us -> none
    pallas_call x1, Pallas kernels: 28.3 us -> 27.9 us  [local(): pl.pallas_call(functools.partial(kernel, nt, nr, reduce_here), out_shape=...]
where the time goes in v2:
time: 39.5 us; the launch traced here: 39.3 us
  Pallas kernels  38.7 us (98%)
  between operations  0.64 us (2%)
    pallas_call x1, Pallas kernels, local(): pl.pallas_call(functools.partial(kernel, nt, nr, reduce_here), out_shape=...  27.9 us
    pallas_call x1, Pallas kernels, local(): pl.pallas_call(deliver, out_shape=tuple((jax.ShapeDtypeStruct(x.shape, x....  10.8 us

profile of v2, /device:TPU:0, one launch (start us, length us, event | category | flops | bytes accessed | tf_op | source)
XLA Modules:
  0.0 39.3 jit_solution(17164453864951866734)
XLA Ops:
  0.6 27.9 %conv_silu_grads.1 = (bf16[2,2,128,128]{3,2,1,0:T(8,128)(2,1)}, bf16[2,2,128,128]{3,2,1,0:T(8,128)(2,1)}, f32[16,864]{1,0:T(8,128)}) custom-call(bf16[2,2,128,128]{3,2,1,0:T(8,128)(2,1)} %video.1, bf16[9,384,128]{2,1,0:T(8,128)(2,1)} %bitcast.1, bf16[2,2,128,128]{3,2,1,0:T(8,128)(2,1)} %cot.1), custom_call_target="tpu_custom_call" | custom-call | flops 1358954496 | bytes 4194304 | tf_op jit(solution)/shard_map/conv_silu_grads/pallas_call | solution.py:386
  28.5 10.8 %deliver.1 = (bf16[2,2,128,128]{3,2,1,0:T(8,128)(2,1)}, bf16[2,2,128,128]{3,2,1,0:T(8,128)(2,1)}, f32[16,864]{1,0:T(8,128)}) custom-call(bf16[2,2,128,128]{3,2,1,0:T(8,128)(2,1)} %get-tuple-element.6.refs_0_, bf16[2,2,128,128]{3,2,1,0:T(8,128)(2,1)} %get-tuple-element.7.refs_1_, f32[16,864]{1,0:T(8,128)} %get-tuple-element.8.refs_2_), custom_call_target="tpu_custom_call" | custom-call | tf_op jit(solution)/shard_map/deliver/pallas_call | solution.py:409

commit v3 on v2

--- a/solution.py
+++ b/solution.py
@@ -10,7 +10,7 @@
 MESH = pl.DeviceIdType.MESH
 F32 = jnp.float32
 BF16 = jnp.bfloat16
-VMEM_BYTES = 56 * 1024 * 1024
+VMEM_BYTES = (53 * 1024 + 576) * 1024
 
 
 def along_width(lines, width):
@@ -409,10 +409,10 @@
     return pl.pallas_call(
         deliver,
         out_shape=tuple(jax.ShapeDtypeStruct(x.shape, x.dtype) for x in results),
-        in_specs=[far] * 3,
+        in_specs=[pl.BlockSpec(memory_space=pltpu.VMEM)] * 3,
         out_specs=(far,) * 3,
         scratch_shapes=[pltpu.SemaphoreType.DMA((3,))],
-        compiler_params=pltpu.CompilerParams(vmem_limit_bytes=VMEM_BYTES),
+        compiler_params=pltpu.CompilerParams(vmem_limit_bytes=4 * 1024 * 1024),
         name="deliver",
     )(*results)
 

time: 39.5 us -> 29.1 us (0.74)
  Pallas kernels: 38.7 us -> 28.3 us
    pallas_call x1, Pallas kernels: 10.8 us -> 0.74 us  [local(): pl.pallas_call(deliver, out_shape=tuple((jax.ShapeDtypeStruct(x.shape, x....]
where the time goes in v3:
time: 29.1 us; the launch traced here: 28.9 us
  Pallas kernels  28.3 us (97%)
  between operations  0.64 us (2%)
    pallas_call x1, Pallas kernels, local(): pl.pallas_call(functools.partial(kernel, nt, nr, reduce_here), out_shape=...  27.6 us
    pallas_call x1, Pallas kernels, local(): pl.pallas_call(deliver, out_shape=tuple((jax.ShapeDtypeStruct(x.shape, x....  0.74 us

profile of v3, /device:TPU:0, one launch (start us, length us, event | category | flops | bytes accessed | tf_op | source)
XLA Modules:
  0.0 28.9 jit_solution(8941431302950749202)
XLA Ops:
  0.6 27.6 %conv_silu_grads.1 = (bf16[2,2,128,128]{3,2,1,0:T(8,128)(2,1)S(1)}, bf16[2,2,128,128]{3,2,1,0:T(8,128)(2,1)S(1)}, f32[16,864]{1,0:T(8,128)S(1)}) custom-call(bf16[2,2,128,128]{3,2,1,0:T(8,128)(2,1)} %video.1, bf16[9,384,128]{2,1,0:T(8,128)(2,1)} %bitcast.1, bf16[2,2,128,128]{3,2,1,0:T(8,128)(2,1)} %cot.1), custom_call_target="tpu_custom_call" | custom-call | flops 1358954496 | bytes 4194304 | tf_op jit(solution)/shard_map/conv_silu_grads/pallas_call | solution.py:386
  28.2 0.7 %deliver.1 = (bf16[2,2,128,128]{3,2,1,0:T(8,128)(2,1)}, bf16[2,2,128,128]{3,2,1,0:T(8,128)(2,1)}, f32[16,864]{1,0:T(8,128)}) custom-call(bf16[2,2,128,128]{3,2,1,0:T(8,128)(2,1)S(1)} %get-tuple-element.6.refs_0_, bf16[2,2,128,128]{3,2,1,0:T(8,128)(2,1)S(1)} %get-tuple-element.7.refs_1_, f32[16,864]{1,0:T(8,128)S(1)} %get-tuple-element.8.refs_2_), custom_call_target="tpu_custom_call" | custom-call | tf_op jit(solution)/shard_map/deliver/pallas_call | solution.py:409

commit v4 on v3

--- a/solution.py
+++ b/solution.py
@@ -28,8 +28,8 @@
 
 def kernel(
     nt, nr, reduce_here,
-    video, weights, cot, act_out, igrad_out, kgrad_out,
-    act, igrad, kgrad, taps, cot_own, seen, patches, gext, gpatches, total, chunks,
+    video, weights, cot, act, igrad, kgrad,
+    taps, cot_own, seen, patches, gext, gpatches, total, chunks,
     s0, r0, a1, s1a, r1a, s1b, r1b, a2a, a2b, s2a, r2a, s2b, r2b, a3, s3, r3,
     local_sem, vsend, vrecv, gsend, grecv, ksend, krecv,
 ):
@@ -162,12 +162,6 @@
     sig = 1.0 / (1.0 + jnp.exp(-pre))
     act[...] = (pre * sig).astype(BF16).reshape(act.shape)
     loads[2].wait()
-    stores = [
-        pltpu.make_async_copy(act, act_out, local_sem.at[3]),
-        pltpu.make_async_copy(igrad, igrad_out, local_sem.at[4]),
-        pltpu.make_async_copy(kgrad, kgrad_out, local_sem.at[5]),
-    ]
-    stores[0].start()
     cot_flat = cot_own[...].reshape(rows, chans).astype(F32)
     grad = (cot_flat * sig * (1.0 + pre * (1.0 - sig))).astype(BF16)
     mine, later = pl.ds(0, frames), pl.ds(frames, 2)
@@ -228,19 +222,15 @@
         spread(gpatches, later, bottom, gext[later, bottom])
         out = out + backward(1, 2) + backward(2, 2)
         igrad[...] = out.astype(BF16).reshape(igrad.shape)
-        stores[1].start()
 
     def finish():
         for part in halo + passed + ghalo:
             sent(part)
-        for store in stores:
-            store.wait()
 
     if not reduce_here:
         for k in range(9):
             weight_part(k)
         kgrad[...] = total[...]
-        stores[2].start()
         out = grad_later(grad_own())
         grad_rows()
         grad_corners(grad_edges(out))
@@ -290,6 +280,7 @@
     s1b[...] = a1[:, 2:4, 1 - side].astype(BF16)
     copies.append(send(3, s1b, r1b, other_side))
 
+    grad_rows()
     out = grad_later(out)
 
     copies[2].wait_recv()
@@ -301,7 +292,6 @@
     s2b[...] = a2b[1 - across].astype(BF16)
     copies.append(send(5, s2b, r2b, other_across))
 
-    grad_rows()
     out = grad_edges(out)
 
     copies[4].wait_recv()
@@ -321,7 +311,6 @@
         copies[5 + k].wait_recv()
         owned = owned + r3[k - 1].astype(F32)
     kgrad[...] = owned[:, :columns]
-    stores[2].start()
     for copy in copies:
         copy.wait_send()
     finish()
@@ -348,9 +337,6 @@
     far = pl.BlockSpec(memory_space=pl.ANY)
     kshape = (share, columns) if reduce_here else (chans, cols)
     scratch = [
-        vm(video.shape, BF16),
-        vm(video.shape, BF16),
-        vm(kshape, F32),
         vm((9, 3 * chans, chans), BF16),
         vm(video.shape, BF16),
         vm((frames + 2, height + 2, width, chans), BF16),
@@ -375,7 +361,7 @@
         vm((4, sh, wide), F32),
         vm((3, sh, wide), BF16),
         vm((3, sh, wide), BF16),
-        pltpu.SemaphoreType.DMA((6,)),
+        pltpu.SemaphoreType.DMA((3,)),
         pltpu.SemaphoreType.DMA((5,)),
         pltpu.SemaphoreType.DMA((5,)),
         pltpu.SemaphoreType.DMA((5,)),
@@ -391,7 +377,7 @@
             jax.ShapeDtypeStruct(kshape, F32),
         ),
         in_specs=[far, far, far],
-        out_specs=(far, far, far),
+        out_specs=(pl.BlockSpec(memory_space=pltpu.VMEM),) * 3,
         scratch_shapes=scratch,
         compiler_params=pltpu.CompilerParams(
             collective_id=0, has_side_effects=True, vmem_limit_bytes=VMEM_BYTES

time: 29.1 us -> 28.3 us (0.973)
  Pallas kernels: 28.3 us -> 27.5 us
    pallas_call x1, Pallas kernels: 27.6 us -> 26.8 us  [local(): pl.pallas_call(functools.partial(kernel, nt, nr, reduce_here), out_shape=...]
where the time goes in v4:
time: 28.3 us; the launch traced here: 28.1 us
  Pallas kernels  27.5 us (97%)
  between operations  0.64 us (2%)
    pallas_call x1, Pallas kernels, local(): pl.pallas_call(functools.partial(kernel, nt, nr, reduce_here), out_shape=...  26.8 us
    pallas_call x1, Pallas kernels, local(): pl.pallas_call(deliver, out_shape=tuple((jax.ShapeDtypeStruct(x.shape, x....  0.74 us

profile of v4, /device:TPU:0, one launch (start us, length us, event | category | flops | bytes accessed | tf_op | source)
XLA Modules:
  0.0 28.1 jit_solution(12758212980749557617)
XLA Ops:
  0.6 26.8 %conv_silu_grads.1 = (bf16[2,2,128,128]{3,2,1,0:T(8,128)(2,1)S(1)}, bf16[2,2,128,128]{3,2,1,0:T(8,128)(2,1)S(1)}, f32[16,864]{1,0:T(8,128)S(1)}) custom-call(bf16[2,2,128,128]{3,2,1,0:T(8,128)(2,1)} %video.1, bf16[9,384,128]{2,1,0:T(8,128)(2,1)} %bitcast.1, bf16[2,2,128,128]{3,2,1,0:T(8,128)(2,1)} %cot.1), custom_call_target="tpu_custom_call" | custom-call | flops 1358954496 | bytes 4194304 | tf_op jit(solution)/shard_map/conv_silu_grads/pallas_call | solution.py:372
  27.4 0.7 %deliver.1 = (bf16[2,2,128,128]{3,2,1,0:T(8,128)(2,1)}, bf16[2,2,128,128]{3,2,1,0:T(8,128)(2,1)}, f32[16,864]{1,0:T(8,128)}) custom-call(bf16[2,2,128,128]{3,2,1,0:T(8,128)(2,1)S(1)} %get-tuple-element.6.refs_0_, bf16[2,2,128,128]{3,2,1,0:T(8,128)(2,1)S(1)} %get-tuple-element.7.refs_1_, f32[16,864]{1,0:T(8,128)S(1)} %get-tuple-element.8.refs_2_), custom_call_target="tpu_custom_call" | custom-call | tf_op jit(solution)/shard_map/deliver/pallas_call | solution.py:395

commit v5 on v4

--- a/solution.py
+++ b/solution.py
@@ -30,7 +30,7 @@
     nt, nr, reduce_here,
     video, weights, cot, act, igrad, kgrad,
     taps, cot_own, seen, patches, gext, gpatches, total, chunks,
-    s0, r0, a1, s1a, r1a, s1b, r1b, a2a, a2b, s2a, r2a, s2b, r2b, a3, s3, r3,
+    s0, r0, s1a, r1a, s1b, r1b, s2a, r2a, s2b, r2b, a3, s3, r3,
     local_sem, vsend, vrecv, gsend, grecv, ksend, krecv,
 ):
     frames, height, width, chans = video.shape
@@ -92,8 +92,8 @@
         )
         return (copy, send_when)
 
-    def start(part):
-        pl.when(part[1])(part[0].start)
+    def start(part, also=True):
+        pl.when(part[1] & also)(part[0].start)
 
     def sent(part):
         pl.when(part[1])(part[0].wait_send)
@@ -115,9 +115,10 @@
         piece(1, 1, inside(1, 1) & odd, video.at[last, height - 1], seen.at[old, top], vsems, 3),
         piece(1, -1, inside(1, -1) & odd, video.at[last, 0], seen.at[old, bottom], vsems, 4),
     ]
-    for part in halo:
-        start(part)
     even = jnp.logical_not(odd)
+    start(halo[0])
+    start(halo[1], even)
+    start(halo[2], even)
     newest = pl.ds(frames, 2)
     passed = [
         piece(1, 0, inside(1, -1) & even, seen.at[newest, top], seen.at[old, top], vsems, 3),
@@ -137,6 +138,10 @@
 
     loads[0].wait()
     spread(patches, new, own, seen[new, own])
+    start(halo[1], odd)
+    start(halo[2], odd)
+    start(halo[3])
+    start(halo[4])
     loads[1].wait()
     pre = forward(2, 1)
     arrive(halo[0], -1, 0, seen.at[old, own])
@@ -258,46 +263,69 @@
         copy.start()
         return copy
 
-    copies = []
+    halves = [
+        pltpu.make_async_remote_copy(
+            src_ref=s0.at[half], dst_ref=r0.at[half],
+            send_sem=ksend.at[half], recv_sem=krecv.at[half],
+            device_id=other_core, device_id_type=MESH,
+        )
+        for half in range(2)
+    ]
+    copies = list(halves)
     done = 0
-    for half in range(2):
-        need = -(-columns * (2 * half + 2) // kdepth)
+    for j in range(nt):
+        need = -(-columns * (j + 1) // kdepth)
         for k in range(done, need):
             weight_part(k)
         done = need
-        cut(2 * half)
-        cut(2 * half + 1)
-        s0[half] = chunks[2 * half + 1 - core].astype(BF16)
-        copies.append(send(half, s0.at[half], r0.at[half], other_core))
+        cut(j)
+
+        @pl.when(core != j % 2)
+        def _(j=j):
+            s0[j // 2] = chunks[j].astype(BF16)
+            halves[j // 2].start()
 
     out = grad_own()
 
+    near, away = across * 2 + core, (1 - across) * 2 + core
+    for half in halves:
+        half.wait_recv()
+    s1a[...] = (chunks[away, 0:2] + r0[1 - across, 0:2].astype(F32)).astype(BF16)
+    copies.append(send(2, s1a, r1a, other_across))
     for half in range(2):
-        copies[half].wait_recv()
-        a1[half] = chunks[2 * half + core] + r0[half].astype(F32)
-    s1a[...] = a1[1 - across, 0:2].astype(BF16)
-    copies.append(send(2, s1a, r1a, other_across))
-    s1b[...] = a1[:, 2:4, 1 - side].astype(BF16)
+        s1b[half] = (
+            chunks[half * 2 + core, 2:4, 1 - side] + r0[half, 2:4, 1 - side].astype(F32)
+        ).astype(BF16)
     copies.append(send(3, s1b, r1b, other_side))
 
     grad_rows()
     out = grad_later(out)
 
     copies[2].wait_recv()
-    a2a[...] = a1[across, 0:2] + r1a[...].astype(F32)
-    s2a[...] = a2a[:, 1 - side].astype(BF16)
+    s2a[...] = (
+        chunks[near, 0:2, 1 - side] + r0[across, 0:2, 1 - side].astype(F32)
+        + r1a[:, 1 - side].astype(F32)
+    ).astype(BF16)
     copies.append(send(4, s2a, r2a, other_side))
     copies[3].wait_recv()
-    a2b[...] = a1[:, 2:4, side] + r1b[...].astype(F32)
-    s2b[...] = a2b[1 - across].astype(BF16)
+    s2b[...] = (
+        chunks[away, 2:4, side] + r0[1 - across, 2:4, side].astype(F32)
+        + r1b[1 - across].astype(F32)
+    ).astype(BF16)
     copies.append(send(5, s2b, r2b, other_across))
+    a3[0:2] = (
+        chunks[near, 0:2, side] + r0[across, 0:2, side].astype(F32) + r1a[:, side].astype(F32)
+    )
+    a3[2:4] = (
+        chunks[near, 2:4, side] + r0[across, 2:4, side].astype(F32) + r1b[across].astype(F32)
+    )
 
     out = grad_edges(out)
 
     copies[4].wait_recv()
-    a3[0:2] = a2a[:, side] + r2a[...].astype(F32)
+    a3[0:2] = a3[0:2] + r2a[...].astype(F32)
     copies[5].wait_recv()
-    a3[2:4] = a2b[across] + r2b[...].astype(F32)
+    a3[2:4] = a3[2:4] + r2b[...].astype(F32)
     for k in (1, 2, 3):
         s3[k - 1] = a3[layers[k]].astype(BF16)
         copies.append(
@@ -347,13 +375,10 @@
         vm((4, 4, 2, sh, wide), F32),
         vm((2, 4, 2, sh, wide), BF16),
         vm((2, 4, 2, sh, wide), BF16),
-        vm((2, 4, 2, sh, wide), F32),
         vm((2, 2, sh, wide), BF16),
         vm((2, 2, sh, wide), BF16),
         vm((2, 2, sh, wide), BF16),
         vm((2, 2, sh, wide), BF16),
-        vm((2, 2, sh, wide), F32),
-        vm((2, 2, sh, wide), F32),
         vm((2, sh, wide), BF16),
         vm((2, sh, wide), BF16),
         vm((2, sh, wide), BF16),

time: 28.3 us -> 28.8 us (1.018)
  Pallas kernels: 27.5 us -> 28 us
    pallas_call x1, Pallas kernels: 26.8 us -> 27.3 us  [local(): pl.pallas_call(functools.partial(kernel, nt, nr, reduce_here), out_shape=...]
where the time goes in v5:
time: 28.8 us; the launch traced here: 28.6 us
  Pallas kernels  28 us (97%)
  between operations  0.64 us (2%)
    pallas_call x1, Pallas kernels, local(): pl.pallas_call(functools.partial(kernel, nt, nr, reduce_here), out_shape=...  27.3 us
    pallas_call x1, Pallas kernels, local(): pl.pallas_call(deliver, out_shape=tuple((jax.ShapeDtypeStruct(x.shape, x....  0.74 us

profile of v5, /device:TPU:0, one launch (start us, length us, event | category | flops | bytes accessed | tf_op | source)
XLA Modules:
  0.0 28.6 jit_solution(11760508408581079664)
XLA Ops:
  0.6 27.3 %conv_silu_grads.1 = (bf16[2,2,128,128]{3,2,1,0:T(8,128)(2,1)S(1)}, bf16[2,2,128,128]{3,2,1,0:T(8,128)(2,1)S(1)}, f32[16,864]{1,0:T(8,128)S(1)}) custom-call(bf16[2,2,128,128]{3,2,1,0:T(8,128)(2,1)} %video.1, bf16[9,384,128]{2,1,0:T(8,128)(2,1)} %bitcast.1, bf16[2,2,128,128]{3,2,1,0:T(8,128)(2,1)} %cot.1), custom_call_target="tpu_custom_call" | custom-call | flops 1358954496 | bytes 4194304 | tf_op jit(solution)/shard_map/conv_silu_grads/pallas_call | solution.py:397
  27.9 0.7 %deliver.1 = (bf16[2,2,128,128]{3,2,1,0:T(8,128)(2,1)}, bf16[2,2,128,128]{3,2,1,0:T(8,128)(2,1)}, f32[16,864]{1,0:T(8,128)}) custom-call(bf16[2,2,128,128]{3,2,1,0:T(8,128)(2,1)S(1)} %get-tuple-element.6.refs_0_, bf16[2,2,128,128]{3,2,1,0:T(8,128)(2,1)S(1)} %get-tuple-element.7.refs_1_, f32[16,864]{1,0:T(8,128)S(1)} %get-tuple-element.8.refs_2_), custom_call_target="tpu_custom_call" | custom-call | tf_op jit(solution)/shard_map/deliver/pallas_call | solution.py:420

commit v6 on v5

--- a/solution.py
+++ b/solution.py
@@ -55,14 +55,13 @@
         load.start()
 
     barrier = pltpu.get_barrier_semaphore()
-    odd = lax.rem(tm, 2) == 1
     around = [(dt, dr) for dt in (-1, 0, 1) for dr in (-1, 0, 1) if dt or dr]
     expected = 0
     for dt, dr in around:
         greets = copies_to = inside(dt, dr)
         if dt and dr:
-            greets = greets & (dt == -1) & jnp.logical_not(odd)
-            copies_to = copies_to & (dt == 1) & odd
+            greets = greets & (dt == -1)
+            copies_to = copies_to & (dt == 1)
         expected = expected + jnp.where(copies_to, 1, 0)
 
         @pl.when(greets)
@@ -92,8 +91,8 @@
         )
         return (copy, send_when)
 
-    def start(part, also=True):
-        pl.when(part[1] & also)(part[0].start)
+    def start(part):
+        pl.when(part[1])(part[0].start)
 
     def sent(part):
         pl.when(part[1])(part[0].wait_send)
@@ -112,18 +111,11 @@
         piece(1, 0, inside(1, 0), video.at[last], seen.at[old, own], vsems, 0),
         piece(0, 1, inside(0, 1), video.at[:, height - 1], seen.at[new, top], vsems, 1),
         piece(0, -1, inside(0, -1), video.at[:, 0], seen.at[new, bottom], vsems, 2),
-        piece(1, 1, inside(1, 1) & odd, video.at[last, height - 1], seen.at[old, top], vsems, 3),
-        piece(1, -1, inside(1, -1) & odd, video.at[last, 0], seen.at[old, bottom], vsems, 4),
+        piece(1, 1, inside(1, 1), video.at[last, height - 1], seen.at[old, top], vsems, 3),
+        piece(1, -1, inside(1, -1), video.at[last, 0], seen.at[old, bottom], vsems, 4),
     ]
-    even = jnp.logical_not(odd)
-    start(halo[0])
-    start(halo[1], even)
-    start(halo[2], even)
-    newest = pl.ds(frames, 2)
-    passed = [
-        piece(1, 0, inside(1, -1) & even, seen.at[newest, top], seen.at[old, top], vsems, 3),
-        piece(1, 0, inside(1, 1) & even, seen.at[newest, bottom], seen.at[old, bottom], vsems, 4),
-    ]
+    for part in halo:
+        start(part)
 
     def spread(target, fr, ro, lines):
         flat = lines.reshape((-1,) + lines.shape[-2:])
@@ -138,10 +130,6 @@
 
     loads[0].wait()
     spread(patches, new, own, seen[new, own])
-    start(halo[1], odd)
-    start(halo[2], odd)
-    start(halo[3])
-    start(halo[4])
     loads[1].wait()
     pre = forward(2, 1)
     arrive(halo[0], -1, 0, seen.at[old, own])
@@ -149,9 +137,7 @@
     pre = pre + forward(0, 1)
     pre = pre + forward(1, 1)
     arrive(halo[1], 0, -1, seen.at[new, top])
-    start(passed[0])
     arrive(halo[2], 0, 1, seen.at[new, bottom])
-    start(passed[1])
     spread(patches, new, top, seen[new, top])
     spread(patches, new, bottom, seen[new, bottom])
     pre = pre + forward(2, 0)
@@ -229,7 +215,7 @@
         igrad[...] = out.astype(BF16).reshape(igrad.shape)
 
     def finish():
-        for part in halo + passed + ghalo:
+        for part in halo + ghalo:
             sent(part)
 
     if not reduce_here:

time: 28.8 us -> 29.2 us (1.014)
  Pallas kernels: 28 us -> 28.4 us
    pallas_call x1, Pallas kernels: 27.3 us -> 27.7 us  [local(): pl.pallas_call(functools.partial(kernel, nt, nr, reduce_here), out_shape=...]
where the time goes in v6:
time: 29.2 us; the launch traced here: 29 us
  Pallas kernels  28.4 us (97%)
  between operations  0.64 us (2%)
    pallas_call x1, Pallas kernels, local(): pl.pallas_call(functools.partial(kernel, nt, nr, reduce_here), out_shape=...  27.7 us
    pallas_call x1, Pallas kernels, local(): pl.pallas_call(deliver, out_shape=tuple((jax.ShapeDtypeStruct(x.shape, x....  0.74 us

profile of v6, /device:TPU:0, one launch (start us, length us, event | category | flops | bytes accessed | tf_op | source)
XLA Modules:
  0.0 29.0 jit_solution(17587270588855444739)
XLA Ops:
  0.6 27.7 %conv_silu_grads.1 = (bf16[2,2,128,128]{3,2,1,0:T(8,128)(2,1)S(1)}, bf16[2,2,128,128]{3,2,1,0:T(8,128)(2,1)S(1)}, f32[16,864]{1,0:T(8,128)S(1)}) custom-call(bf16[2,2,128,128]{3,2,1,0:T(8,128)(2,1)} %video.1, bf16[9,384,128]{2,1,0:T(8,128)(2,1)} %bitcast.1, bf16[2,2,128,128]{3,2,1,0:T(8,128)(2,1)} %cot.1), custom_call_target="tpu_custom_call" | custom-call | flops 1358954496 | bytes 4194304 | tf_op jit(solution)/shard_map/conv_silu_grads/pallas_call | solution.py:383
  28.3 0.7 %deliver.1 = (bf16[2,2,128,128]{3,2,1,0:T(8,128)(2,1)}, bf16[2,2,128,128]{3,2,1,0:T(8,128)(2,1)}, f32[16,864]{1,0:T(8,128)}) custom-call(bf16[2,2,128,128]{3,2,1,0:T(8,128)(2,1)S(1)} %get-tuple-element.6.refs_0_, bf16[2,2,128,128]{3,2,1,0:T(8,128)(2,1)S(1)} %get-tuple-element.7.refs_1_, f32[16,864]{1,0:T(8,128)S(1)} %get-tuple-element.8.refs_2_), custom_call_target="tpu_custom_call" | custom-call | tf_op jit(solution)/shard_map/deliver/pallas_call | solution.py:406

commit v7 on v4

--- a/solution.py
+++ b/solution.py
@@ -92,8 +92,8 @@
         )
         return (copy, send_when)
 
-    def start(part):
-        pl.when(part[1])(part[0].start)
+    def start(part, also=True):
+        pl.when(part[1] & also)(part[0].start)
 
     def sent(part):
         pl.when(part[1])(part[0].wait_send)
@@ -174,8 +174,9 @@
         piece(-1, 0, inside(-1, -1), gext.at[early, top], gext.at[later, top], gsems, 3),
         piece(-1, 0, inside(-1, 1), gext.at[early, bottom], gext.at[later, bottom], gsems, 4),
     ]
-    for part in ghalo[:3]:
-        start(part)
+    start(ghalo[0], even if reduce_here else True)
+    start(ghalo[1])
+    start(ghalo[2])
 
     turned = grad.astype(F32).T.astype(BF16)
     kdepth = 3 * chans
@@ -280,8 +281,9 @@
     s1b[...] = a1[:, 2:4, 1 - side].astype(BF16)
     copies.append(send(3, s1b, r1b, other_side))
 
+    start(ghalo[0], odd)
     grad_rows()
-    out = grad_later(out)
+    out = grad_edges(out)
 
     copies[2].wait_recv()
     a2a[...] = a1[across, 0:2] + r1a[...].astype(F32)
@@ -292,7 +294,7 @@
     s2b[...] = a2b[1 - across].astype(BF16)
     copies.append(send(5, s2b, r2b, other_across))
 
-    out = grad_edges(out)
+    out = grad_later(out)
 
     copies[4].wait_recv()
     a3[0:2] = a2a[:, side] + r2a[...].astype(F32)

time: 28.3 us -> 28.3 us (level)
  no operation moved by 1% of the time
where the time goes in v7:
time: 28.3 us; the launch traced here: 28.2 us
  Pallas kernels  27.5 us (97%)
  between operations  0.64 us (2%)
    pallas_call x1, Pallas kernels, local(): pl.pallas_call(functools.partial(kernel, nt, nr, reduce_here), out_shape=...  26.8 us
    pallas_call x1, Pallas kernels, local(): pl.pallas_call(deliver, out_shape=tuple((jax.ShapeDtypeStruct(x.shape, x....  0.74 us

profile of v7, /device:TPU:0, one launch (start us, length us, event | category | flops | bytes accessed | tf_op | source)
XLA Modules:
  0.0 28.2 jit_solution(7272314416706974399)
XLA Ops:
  0.6 26.8 %conv_silu_grads.1 = (bf16[2,2,128,128]{3,2,1,0:T(8,128)(2,1)S(1)}, bf16[2,2,128,128]{3,2,1,0:T(8,128)(2,1)S(1)}, f32[16,864]{1,0:T(8,128)S(1)}) custom-call(bf16[2,2,128,128]{3,2,1,0:T(8,128)(2,1)} %video.1, bf16[9,384,128]{2,1,0:T(8,128)(2,1)} %bitcast.1, bf16[2,2,128,128]{3,2,1,0:T(8,128)(2,1)} %cot.1), custom_call_target="tpu_custom_call" | custom-call | flops 1358954496 | bytes 4194304 | tf_op jit(solution)/shard_map/conv_silu_grads/pallas_call | solution.py:374
  27.4 0.7 %deliver.1 = (bf16[2,2,128,128]{3,2,1,0:T(8,128)(2,1)}, bf16[2,2,128,128]{3,2,1,0:T(8,128)(2,1)}, f32[16,864]{1,0:T(8,128)}) custom-call(bf16[2,2,128,128]{3,2,1,0:T(8,128)(2,1)S(1)} %get-tuple-element.6.refs_0_, bf16[2,2,128,128]{3,2,1,0:T(8,128)(2,1)S(1)} %get-tuple-element.7.refs_1_, f32[16,864]{1,0:T(8,128)S(1)} %get-tuple-element.8.refs_2_), custom_call_target="tpu_custom_call" | custom-call | tf_op jit(solution)/shard_map/deliver/pallas_call | solution.py:397

commit v8 on v5

--- a/solution.py
+++ b/solution.py
@@ -92,8 +92,8 @@
         )
         return (copy, send_when)
 
-    def start(part, also=True):
-        pl.when(part[1] & also)(part[0].start)
+    def start(part):
+        pl.when(part[1])(part[0].start)
 
     def sent(part):
         pl.when(part[1])(part[0].wait_send)
@@ -116,9 +116,8 @@
         piece(1, -1, inside(1, -1) & odd, video.at[last, 0], seen.at[old, bottom], vsems, 4),
     ]
     even = jnp.logical_not(odd)
-    start(halo[0])
-    start(halo[1], even)
-    start(halo[2], even)
+    for part in halo:
+        start(part)
     newest = pl.ds(frames, 2)
     passed = [
         piece(1, 0, inside(1, -1) & even, seen.at[newest, top], seen.at[old, top], vsems, 3),
@@ -138,10 +137,6 @@
 
     loads[0].wait()
     spread(patches, new, own, seen[new, own])
-    start(halo[1], odd)
-    start(halo[2], odd)
-    start(halo[3])
-    start(halo[4])
     loads[1].wait()
     pre = forward(2, 1)
     arrive(halo[0], -1, 0, seen.at[old, own])

time: 28.8 us -> 28.5 us (0.990)
  Pallas kernels: 28 us -> 27.7 us
    pallas_call x1, Pallas kernels: 27.3 us -> 27 us  [local(): pl.pallas_call(functools.partial(kernel, nt, nr, reduce_here), out_shape=...]
where the time goes in v8:
time: 28.5 us; the launch traced here: 28.3 us
  Pallas kernels  27.7 us (97%)
  between operations  0.64 us (2%)
    pallas_call x1, Pallas kernels, local(): pl.pallas_call(functools.partial(kernel, nt, nr, reduce_here), out_shape=...  27 us
    pallas_call x1, Pallas kernels, local(): pl.pallas_call(deliver, out_shape=tuple((jax.ShapeDtypeStruct(x.shape, x....  0.74 us

profile of v8, /device:TPU:0, one launch (start us, length us, event | category | flops | bytes accessed | tf_op | source)
XLA Modules:
  0.0 28.3 jit_solution(13113138456216649218)
XLA Ops:
  0.6 27.0 %conv_silu_grads.1 = (bf16[2,2,128,128]{3,2,1,0:T(8,128)(2,1)S(1)}, bf16[2,2,128,128]{3,2,1,0:T(8,128)(2,1)S(1)}, f32[16,864]{1,0:T(8,128)S(1)}) custom-call(bf16[2,2,128,128]{3,2,1,0:T(8,128)(2,1)} %video.1, bf16[9,384,128]{2,1,0:T(8,128)(2,1)} %bitcast.1, bf16[2,2,128,128]{3,2,1,0:T(8,128)(2,1)} %cot.1), custom_call_target="tpu_custom_call" | custom-call | flops 1358954496 | bytes 4194304 | tf_op jit(solution)/shard_map/conv_silu_grads/pallas_call | solution.py:392
  27.6 0.7 %deliver.1 = (bf16[2,2,128,128]{3,2,1,0:T(8,128)(2,1)}, bf16[2,2,128,128]{3,2,1,0:T(8,128)(2,1)}, f32[16,864]{1,0:T(8,128)}) custom-call(bf16[2,2,128,128]{3,2,1,0:T(8,128)(2,1)S(1)} %get-tuple-element.6.refs_0_, bf16[2,2,128,128]{3,2,1,0:T(8,128)(2,1)S(1)} %get-tuple-element.7.refs_1_, f32[16,864]{1,0:T(8,128)S(1)} %get-tuple-element.8.refs_2_), custom_call_target="tpu_custom_call" | custom-call | tf_op jit(solution)/shard_map/deliver/pallas_call | solution.py:415

commit v9 on v4

--- a/solution.py
+++ b/solution.py
@@ -132,32 +132,30 @@
     def patch(source, a, b):
         return source[a:a + frames, b:b + height].reshape(rows, 3 * chans)
 
-    def forward(a, b):
-        return jnp.dot(patch(patches, a, b), taps[a * 3 + b], preferred_element_type=F32)
+    def forward(*at):
+        lines = jnp.concatenate([patch(patches, a, b) for a, b in at], axis=1)
+        mat = jnp.concatenate([taps[a * 3 + b] for a, b in at], axis=0)
+        return jnp.dot(lines, mat, preferred_element_type=F32)
 
     loads[0].wait()
     spread(patches, new, own, seen[new, own])
     loads[1].wait()
-    pre = forward(2, 1)
+    pre = forward((2, 1))
     arrive(halo[0], -1, 0, seen.at[old, own])
     spread(patches, old, own, seen[old, own])
-    pre = pre + forward(0, 1)
-    pre = pre + forward(1, 1)
+    pre = pre + forward((0, 1), (1, 1))
     arrive(halo[1], 0, -1, seen.at[new, top])
     start(passed[0])
     arrive(halo[2], 0, 1, seen.at[new, bottom])
     start(passed[1])
     spread(patches, new, top, seen[new, top])
     spread(patches, new, bottom, seen[new, bottom])
-    pre = pre + forward(2, 0)
-    pre = pre + forward(2, 2)
+    pre = pre + forward((2, 0), (2, 2))
     arrive(halo[3], -1, -1, seen.at[old, top])
     spread(patches, old, top, seen[old, top])
     arrive(halo[4], -1, 1, seen.at[old, bottom])
     spread(patches, old, bottom, seen[old, bottom])
-    for b in (0, 2):
-        for a in range(2):
-            pre = pre + forward(a, b)
+    pre = pre + forward((0, 0), (1, 0), (0, 2), (1, 2))
 
     sig = 1.0 / (1.0 + jnp.exp(-pre))
     act[...] = (pre * sig).astype(BF16).reshape(act.shape)

time: 28.3 us -> 29.1 us (1.028)
  Pallas kernels: 27.5 us -> 28.3 us
    pallas_call x1, Pallas kernels: 26.8 us -> 27.5 us  [local(): pl.pallas_call(functools.partial(kernel, nt, nr, reduce_here), out_shape=...]
where the time goes in v9:
time: 29.1 us; the launch traced here: 28.9 us
  Pallas kernels  28.3 us (97%)
  between operations  0.64 us (2%)
    pallas_call x1, Pallas kernels, local(): pl.pallas_call(functools.partial(kernel, nt, nr, reduce_here), out_shape=...  27.5 us
    pallas_call x1, Pallas kernels, local(): pl.pallas_call(deliver, out_shape=tuple((jax.ShapeDtypeStruct(x.shape, x....  0.74 us

profile of v9, /device:TPU:0, one launch (start us, length us, event | category | flops | bytes accessed | tf_op | source)
XLA Modules:
  0.0 28.9 jit_solution(5468182184262866184)
XLA Ops:
  0.6 27.5 %conv_silu_grads.1 = (bf16[2,2,128,128]{3,2,1,0:T(8,128)(2,1)S(1)}, bf16[2,2,128,128]{3,2,1,0:T(8,128)(2,1)S(1)}, f32[16,864]{1,0:T(8,128)S(1)}) custom-call(bf16[2,2,128,128]{3,2,1,0:T(8,128)(2,1)} %video.1, bf16[9,384,128]{2,1,0:T(8,128)(2,1)} %bitcast.1, bf16[2,2,128,128]{3,2,1,0:T(8,128)(2,1)} %cot.1), custom_call_target="tpu_custom_call" | custom-call | flops 1358954496 | bytes 4194304 | tf_op jit(solution)/shard_map/conv_silu_grads/pallas_call | solution.py:370
  28.2 0.7 %deliver.1 = (bf16[2,2,128,128]{3,2,1,0:T(8,128)(2,1)}, bf16[2,2,128,128]{3,2,1,0:T(8,128)(2,1)}, f32[16,864]{1,0:T(8,128)}) custom-call(bf16[2,2,128,128]{3,2,1,0:T(8,128)(2,1)S(1)} %get-tuple-element.6.refs_0_, bf16[2,2,128,128]{3,2,1,0:T(8,128)(2,1)S(1)} %get-tuple-element.7.refs_1_, f32[16,864]{1,0:T(8,128)S(1)} %get-tuple-element.8.refs_2_), custom_call_target="tpu_custom_call" | custom-call | tf_op jit(solution)/shard_map/deliver/pallas_call | solution.py:393
